TPU v7x, 32 devices: a whole 2x2x4 slice. The times are simulated.
32 devices in a mesh: parts: 2 (over x), seq: 16 (over z, y, core).
Axes of the slice: x: 2, y: 2, z: 4, core: 2. Of those that a mesh axis runs over, the one named last changes fastest.
Arguments:
- tokens: bfloat16 [262144, 512], P(('parts', 'seq')), parts along dimension 0, may hold values from -6 to 6
- cotangent: bfloat16 [262144, 512], P(('parts', 'seq')), parts along dimension 0, may hold values from -0.75 to 0.75
- first_factor: bfloat16 [512, 256, 256], P('seq'), may hold values from -0.375 to 0.375
- second_factor: bfloat16 [256, 512, 512], P('seq'), may hold values from -0.25 to 0.25
- gate_weight: bfloat16 [512, 512], replicated, may hold values from -0.25 to 0.25
Outputs:
- token_grad: bfloat16 [262144, 512], P(('parts', 'seq')), parts along dimension 0
- first_grad: bfloat16 [1024, 256, 256], P(('parts', 'seq')), parts along dimension 0
- second_grad: bfloat16 [512, 512, 512], P(('parts', 'seq')), parts along dimension 0
- gate_grad: bfloat16 [1024, 512], P('parts'), parts along dimension 0
There are 2 independent parts, one for each index of `parts`. A program takes and returns all parts, laid end to end along the dimension named above; an argument that names none is the same for every part. Nothing has to cross between parts.
All inputs are finite; a program needn't handle non-finite values.
Results may differ from a plain program's by a relative error of at most 0.0061.
Values may be sent and summed in bfloat16 or wider, within the bound.
A program may use at most 256 MiB of HBM per device.

v0:
```python
import jax
import jax.numpy as jnp
from jax import lax
from jax.sharding import PartitionSpec as P


def on_device(tokens, cotangent, first_factor, second_factor, gate_weight):
    width = tokens.shape[1]
    outer_local = first_factor.shape[0]
    inner_size = first_factor.shape[1]
    inner_local = second_factor.shape[0]
    outer_size = second_factor.shape[1]
    gate = jax.nn.sigmoid(jnp.dot(tokens, gate_weight, preferred_element_type=jnp.float32))
    tok_f = tokens.astype(jnp.float32)
    mixed = (tok_f * gate).astype(jnp.bfloat16)
    mixed3 = mixed.reshape(outer_local, inner_size, width)
    middle = jnp.einsum(
        "abk,akc->bac", first_factor, mixed3, preferred_element_type=jnp.float32
    ).astype(jnp.bfloat16)
    back = cotangent.reshape(inner_local, outer_size, width)
    middle_here = lax.all_to_all(middle, "seq", split_axis=0, concat_axis=1, tiled=True)
    middle_back = jnp.einsum(
        "bak,bac->kbc", second_factor, back, preferred_element_type=jnp.float32
    ).astype(jnp.bfloat16)
    back_here = lax.all_to_all(middle_back, "seq", split_axis=0, concat_axis=1, tiled=True)
    second_grad = jnp.einsum(
        "bac,bkc->bak", back, middle_here, preferred_element_type=jnp.float32
    ).astype(jnp.bfloat16)
    mixed_back = jnp.einsum(
        "abk,abc->akc", first_factor, back_here, preferred_element_type=jnp.float32
    )
    first_grad = jnp.einsum(
        "abc,akc->abk", back_here, mixed3, preferred_element_type=jnp.float32
    ).astype(jnp.bfloat16)
    mixed_back = mixed_back.reshape(outer_local * inner_size, width)
    slope = (mixed_back * tok_f * gate * (1.0 - gate)).astype(jnp.bfloat16)
    token_grad = mixed_back * gate + lax.dot_general(
        slope, gate_weight, (((1,), (1,)), ((), ())), preferred_element_type=jnp.float32
    )
    gate_local = lax.dot_general(
        tokens, slope, (((0,), (0,)), ((), ())), preferred_element_type=jnp.float32
    )
    gate_grad = lax.psum(gate_local, "seq")
    return (
        token_grad.astype(jnp.bfloat16),
        first_grad,
        second_grad,
        gate_grad.astype(jnp.bfloat16),
    )


def solution(mesh):
    return jax.shard_map(
        on_device,
        mesh=mesh,
        in_specs=(
            P(("parts", "seq"), None),
            P(("parts", "seq"), None),
            P("seq", None, None),
            P("seq", None, None),
            P(),
        ),
        out_specs=(
            P(("parts", "seq"), None),
            P(("parts", "seq"), None, None),
            P(("parts", "seq"), None, None),
            P("parts", None),
        ),
        check_vma=False,
    )
```

profile of v0, /device:TPU:0, one launch (start us, length us, event | category | flops | bytes accessed | tf_op | source)
XLA Modules:
  0.0 583.8 jit_solution(12037093897210820653)
XLA Ops:
  0.6 0.0 copy-start
  0.6 11.5 %convert_bitcast_fusion.2 = bf16[512,16,512]{0,2,1:T(8,128)(2,1)} fusion(bf16[16,512,512]{2,1,0:T(8,128)(2,1)} %bitcast.49, bf16[16,512,512]{2,1,0:T(8,128)(2,1)} %param.8), kind=kOutput, calls=%fused_computation.12 | convolution fusion | flops 4299161600 | bytes 25165824 | tf_op jit(solution)/shard_map/bak,bac->kbc/dot_general | solution.py:22
  12.2 14.8 %copy.26 = bf16[512,16,512]{2,1,0:T(8,128)(2,1)} copy(bf16[512,16,512]{0,2,1:T(8,128)(2,1)} %convert_bitcast_fusion.2) | data formatting | bytes 16777216 | tf_op jit(solution)/shard_map/convert_element_type | solution.py:24
  26.9 189.6 %all_to_all.36 = bf16[512,16,512]{2,1,0:T(8,128)(2,1)} all-to-all(bf16[512,16,512]{2,1,0:T(8,128)(2,1)} %copy.26), channel_id=1, replica_groups=mesh['parts'=2,'seq'=16] {'seq'}, dimensions={0} | all-to-all | bytes 16777216 | tf_op jit(solution)/shard_map/all_to_all | solution.py:25
  216.6 8.2 %copy.27 = bf16[32,16,16,512]{3,2,1,0:T(8,128)(2,1)} copy(bf16[32,16,16,512]{3,2,0,1:T(8,128)(2,1)} %bitcast.47) | data formatting | bytes 16777216 | tf_op jit(solution)/shard_map/all_to_all | solution.py:25
  224.8 12.7 %fusion.6 = f32[32,512,256]{1,2,0:T(8,128)} fusion(bf16[32,256,512]{2,1,0:T(8,128)(2,1)} %bitcast.43, bf16[32,256,256]{2,1,0:T(8,128)(2,1)} %param.7), kind=kOutput, calls=%fused_computation.15 | convolution fusion | flops 2147483648 | bytes 29360128 | tf_op jit(solution)/shard_map/abk,abc->akc/dot_general | solution.py:29
  237.5 0.0 copy-done
  237.5 22.4 %fusion.3 = (bf16[8192,512]{1,0:T(8,128)(2,1)S(1)}, bf16[8192,512]{1,0:T(8,128)(2,1)}, f32[8192,512]{1,0:T(8,128)}) fusion(bf16[8192,512]{1,0:T(8,128)(2,1)} %param.5, f32[32,512,256]{1,2,0:T(8,128)} %fusion.6, bf16[512,512]{1,0:T(8,128)(2,1)S(1)} %copy-done), kind=kOutput, calls=%fused_computation.5 | convolution fusion | flops 4341104640 | bytes 59244544 | tf_op jit(solution)/shard_map/dot_general | solution.py:13
  259.9 0.0 copy-start.1
  259.9 3.4 copy-done.1
  263.3 8.0 %convert_bitcast_fusion.1 = bf16[256,32,512]{0,2,1:T(8,128)(2,1)} fusion(bf16[32,256,512]{2,1,0:T(8,128)(2,1)S(1)} %bitcast.45, bf16[32,256,256]{2,1,0:T(8,128)(2,1)} %param.7), kind=kOutput, calls=%fused_computation.11 | convolution fusion | flops 2151677952 | bytes 20971520 | tf_op jit(solution)/shard_map/abk,akc->bac/dot_general | solution.py:17
  271.3 14.6 %copy.30 = bf16[256,32,512]{2,1,0:T(8,128)(2,1)} copy(bf16[256,32,512]{0,2,1:T(8,128)(2,1)} %convert_bitcast_fusion.1) | data formatting | bytes 16777216 | tf_op jit(solution)/shard_map/convert_element_type | solution.py:19
  285.9 5.7 all-to-all-start.1
  291.6 9.5 %convolution_bitcast_fusion = f32[512,512]{0,1:T(8,128)S(1)} fusion(bf16[8192,512]{1,0:T(8,128)(2,1)} %get-tuple-element.17, bf16[8192,512]{1,0:T(8,128)(2,1)} %param.5), kind=kOutput, calls=%fused_computation.14 | convolution fusion | flops 4294967296 | bytes 17825792 | tf_op jit(solution)/shard_map/dot_general | solution.py:40
  301.2 220.4 %all-reduce.1 = bf16[512,512]{0,1:T(8,128)(2,1)S(1)} all-reduce(f32[512,512]{0,1:T(8,128)S(1)} %convolution_bitcast_fusion), channel_id=1, replica_groups=mesh['parts'=2,'seq'=16] {'seq'}, use_global_device_ids=true, to_apply=%region_0.0 | all-reduce | flops 262144 | bytes 1572864 | tf_op jit(solution)/shard_map/psum | solution.py:43
  521.6 1.0 copy.33
  522.6 10.2 %convolution_convert_fusion = bf16[32,256,256]{2,1,0:T(8,128)(2,1)} fusion(bf16[32,256,512]{2,1,0:T(8,128)(2,1)} %bitcast.44, bf16[32,256,512]{2,1,0:T(8,128)(2,1)} %bitcast.46), kind=kOutput, calls=%fused_computation.13 | convolution fusion | flops 2149580800 | bytes 20971520 | tf_op jit(solution)/shard_map/abc,akc->abk/dot_general | solution.py:32
  532.8 18.8 %fusion.5 = bf16[8192,512]{1,0:T(8,128)(2,1)} fusion(f32[8192,512]{1,0:T(8,128)} %get-tuple-element.18, f32[32,512,256]{1,2,0:T(8,128)} %fusion.6, bf16[8192,512]{1,0:T(8,128)(2,1)} %get-tuple-element.17, bf16[512,512]{1,0:T(8,128)(2,1)S(1)} %copy-done), kind=kOutput, calls=%fused_computation.8 | convolution fusion | flops 4307550208 | bytes 50855936 | tf_op jit(solution)/shard_map/dot_general | solution.py:37
  551.6 0.0 all-to-all-done.1
  551.6 8.4 %copy.31 = bf16[16,16,32,512]{3,2,1,0:T(8,128)(2,1)} copy(bf16[16,16,32,512]{3,2,0,1:T(8,128)(2,1)} %bitcast.11) | data formatting | bytes 16777216 | tf_op jit(solution)/shard_map/all_to_all | solution.py:21
  560.0 11.5 %convert_bitcast_fusion = bf16[16,512,512]{1,2,0:T(8,128)(2,1)} fusion(bf16[16,512,512]{2,1,0:T(8,128)(2,1)} %bitcast.48, bf16[16,512,512]{2,1,0:T(8,128)(2,1)} %bitcast.50), kind=kOutput, calls=%fused_computation.10 | convolution fusion | flops 4299161600 | bytes 25165824 | tf_op jit(solution)/shard_map/bac,bkc->bak/dot_general | solution.py:26
  571.5 12.3 %copy.32 = bf16[16,512,512]{2,1,0:T(8,128)(2,1)} copy(bf16[16,512,512]{1,2,0:T(8,128)(2,1)} %convert_bitcast_fusion) | data formatting | bytes 16777216
Async XLA Ops:
  0.6 236.9 %copy-start = (bf16[512,512]{1,0:T(8,128)(2,1)S(1)}, bf16[512,512]{1,0:T(8,128)(2,1)}, u32[]{:S(2)}) copy-start(bf16[512,512]{1,0:T(8,128)(2,1)} %param.9) | copy-start | bytes 1572868
  259.9 3.4 copy-start.1
  285.9 265.7 %all-to-all-start.1 = ((bf16[256,32,512]{2,1,0:T(8,128)(2,1)}), bf16[256,32,512]{2,1,0:T(8,128)(2,1)}, u32[]{:S(2)}, u32[]{:S(2)}) async-start(bf16[256,32,512]{2,1,0:T(8,128)(2,1)} %copy.30), calls=%async_computation.1 | async-start | bytes 16777216 | tf_op jit(solution)/shard_map/all_to_all | solution.py:21
where the time goes:
time: 587 us; the launch traced here: 584 us
  blocking collectives  410 us (70%)
  matrix products  105 us (18%)
  local copies, waits for them, and re-layouts  62.8 us (11%)
    psum x1, blocking collectives, on_device(): gate_grad = lax.psum(gate_local, 'seq')  220 us
    all_to_all x1, blocking collectives, on_device(): lax.all_to_all(middle_back, 'seq', split_axis=0, concat_axis=1, tiled=True)  190 us
    dot_general x1, matrix products, on_device(): jnp.dot(tokens, gate_weight, preferred_element_type=jnp.float32)  22.4 us
    dot_general x1, matrix products, on_device(): lax.dot_general(slope, gate_weight, (((1,), (1,)), ((), ())), preferred_e...  18.8 us
    unnamed x6, local copies, waits for them, and re-layouts  16.7 us
    convert_element_type x1, local copies, waits for them, and re-layouts, on_device(): middle_back = jnp.einsum('bak,bac->kbc', second_factor, back, preferred_e...  14.8 us
    convert_element_type x1, local copies, waits for them, and re-layouts, on_device(): middle = jnp.einsum('abk,akc->bac', first_factor, mixed3, preferred_eleme...  14.6 us
    dot_general x1, matrix products, on_device(): jnp.einsum('abk,abc->akc', first_factor, back_here, preferred_element_typ...  12.7 us
  transfers between devices with their start and end apart: 1, of which 0 were waited for; matrix products, arithmetic and copies ran while one was open for 7% of the time, Pallas kernels for 0%

commit v1 on v0

v1 whole, which is shorter than its diff:
```python
import functools

import jax
import jax.numpy as jnp
from jax import lax
from jax.experimental import pallas as pl
from jax.experimental.pallas import tpu as pltpu
from jax.sharding import PartitionSpec as P

MESH = pl.DeviceIdType.MESH
F32 = jnp.float32
BF16 = jnp.bfloat16
LANES = 128


def dot(x, y, x_dim, y_dim):
    return lax.dot_general(
        x, y, (((x_dim,), (y_dim,)), ((), ())), preferred_element_type=F32
    )


def send_order(n):
    quarters = [list(range(q * n // 4, (q + 1) * n // 4)) for q in (2, 1, 3, 0)]
    order = [s for group in zip(*quarters) for s in group]
    return [s for s in order if s != 0]


def exchange_kernel(
    n, outer, inner, group,
    tok_ref, cot_ref, ff_ref, sf_ref, w_ref,
    tg_ref, fg_ref, gl_ref, mid_recv,
    mb_send, mb_recv, mb_here, mid_group, mid_send,
    mb_out, mb_in, mb_own, mid_out, mid_in, mid_own,
):
    part, me = lax.axis_index("parts"), lax.axis_index("seq")
    step = pl.program_id(0)
    width = tok_ref.shape[2]
    inner_size = tok_ref.shape[1]
    batch = min(4, inner)
    second, third = inner, inner + outer
    last = inner + 2 * outer - 1
    order = send_order(n)

    def all_bytes(send, recv, out_sem, in_sem):
        return pltpu.make_async_remote_copy(
            src_ref=send.at[pl.ds(0, n - 1)], dst_ref=recv.at[pl.ds(0, n - 1)],
            send_sem=out_sem, recv_sem=in_sem,
            device_id=(part, lax.rem(me + 1, n)), device_id_type=MESH,
        )

    mb_all = all_bytes(mb_send, mb_recv, mb_out, mb_in)
    mid_all = all_bytes(mid_send, mid_recv, mid_out, mid_in)
    mb_local = pltpu.make_async_copy(mb_send.at[me], mb_recv.at[me], mb_own)
    mid_local = pltpu.make_async_copy(mid_send.at[me], mid_recv.at[me], mid_own)

    @pl.when(step == 0)
    def _():
        barrier = pltpu.get_barrier_semaphore()
        for s in range(1, n):
            pl.semaphore_signal(
                barrier, inc=1, device_id=(part, lax.rem(me + s, n)), device_id_type=MESH
            )
        pl.semaphore_wait(barrier, n - 1)

    @pl.when(step < second)
    def _():
        made = dot(sf_ref[0], cot_ref[0], 0, 0)
        mb_send[:, step] = made.reshape(n, outer, width).astype(BF16)

        @pl.when(lax.rem(step, batch) == batch - 1)
        def _():
            rows = pl.ds(step - (batch - 1), batch)
            for s in order:
                to = lax.rem(me + s, n)
                pltpu.make_async_remote_copy(
                    src_ref=mb_send.at[to, rows], dst_ref=mb_recv.at[me, rows],
                    send_sem=mb_out, recv_sem=mb_in,
                    device_id=(part, to), device_id_type=MESH,
                ).start()

    @pl.when(step == second)
    def _():
        mb_local.start()

    def gated():
        tok = tok_ref[0]
        tok_f = tok.astype(F32)
        gate = jax.nn.sigmoid(dot(tok, w_ref[...], 1, 0))
        return tok, tok_f, gate, (tok_f * gate).astype(BF16)

    tall = 16 // inner if inner < 16 else 1
    chunk = tall * inner

    @pl.when((step >= second) & (step < third))
    def _():
        at = step - second
        _, _, _, mixed = gated()
        slot = lax.rem(at, group)
        mid_group[slot] = dot(ff_ref[0], mixed, 1, 0).astype(BF16)

        @pl.when(slot == group - 1)
        def _():
            first = pl.multiple_of(at - (group - 1), group)

            def turn(j, carry):
                for c in range(0, width, LANES):
                    cols = pl.ds(c, LANES)
                    rows = pl.ds(pl.multiple_of(j * chunk, chunk), chunk)
                    piece = mid_group[:, rows, cols].astype(F32)
                    piece = jnp.swapaxes(piece, 0, 1).astype(BF16)
                    mid_send[pl.ds(j * tall, tall), :, pl.ds(first, group), cols] = (
                        piece.reshape(tall, inner, group, LANES)
                    )
                return carry

            lax.fori_loop(0, inner_size // chunk, turn, 0)

    @pl.when(step == third - 1)
    def _():
        mb_all.wait_send()
        for s in order:
            to = lax.rem(me + s, n)
            pltpu.make_async_remote_copy(
                src_ref=mid_send.at[to], dst_ref=mid_recv.at[me],
                send_sem=mid_out, recv_sem=mid_in,
                device_id=(part, to), device_id_type=MESH,
            ).start()
        mid_local.start()
        mb_all.wait_recv()
        mb_local.wait()

        def turn(j, carry):
            for c in range(0, width, LANES):
                cols = pl.ds(c, LANES)
                piece = mb_recv[pl.ds(j * tall, tall), :, :, cols]
                piece = piece.reshape(chunk, outer, LANES).astype(F32)
                piece = jnp.swapaxes(piece, 0, 1).astype(BF16)
                rows = pl.ds(pl.multiple_of(j * chunk, chunk), chunk)
                mb_here[:, rows, cols] = piece
            return carry

        lax.fori_loop(0, inner_size // chunk, turn, 0)
        gl_ref[...] = jnp.zeros_like(gl_ref)

    @pl.when(step >= third)
    def _():
        tok, tok_f, gate, mixed = gated()
        back = mb_here[step - third]
        fg_ref[0] = dot(back, mixed, 1, 1).astype(BF16)
        mixed_back = dot(ff_ref[0], back, 0, 0)
        slope = (mixed_back * tok_f * gate * (1.0 - gate)).astype(BF16)
        tg_ref[0] = (mixed_back * gate + dot(slope, w_ref[...], 1, 1)).astype(BF16)
        gl_ref[...] += dot(tok, slope, 0, 0)

    @pl.when(step == last)
    def _():
        mid_all.wait_send()
        mid_all.wait_recv()
        mid_local.wait()


def second_kernel(cot_ref, mid_ref, sg_ref):
    n, _, outer, width = mid_ref.shape
    middle = mid_ref[:, 0]
    if outer % 16:
        middle = middle.astype(F32).reshape(n * outer, width).astype(BF16)
    else:
        middle = middle.reshape(n * outer, width)
    sg_ref[0] = dot(cot_ref[0], middle, 1, 1).astype(BF16)


def on_device(n, tokens, cotangent, first_factor, second_factor, gate_weight):
    width = tokens.shape[1]
    outer, inner_size = first_factor.shape[:2]
    inner, outer_size = second_factor.shape[:2]
    tok3 = tokens.reshape(outer, inner_size, width)
    back = cotangent.reshape(inner, outer_size, width)
    group = min(16, outer)
    steps = inner + 2 * outer

    def by_inner(i):
        return (jnp.minimum(i, inner - 1), 0, 0)

    def by_outer(i):
        return (lax.rem(jnp.maximum(i - inner, 0), outer), 0, 0)

    def by_back(i):
        return (jnp.maximum(i - inner - outer, 0), 0, 0)

    def whole(i):
        return (0, 0)

    moved = (n, inner, outer, width)
    token_grad, first_grad, gate_local, middle_here = pl.pallas_call(
        functools.partial(exchange_kernel, n, outer, inner, group),
        grid=(steps,),
        out_shape=(
            jax.ShapeDtypeStruct(tok3.shape, BF16),
            jax.ShapeDtypeStruct(first_factor.shape, BF16),
            jax.ShapeDtypeStruct(gate_weight.shape, F32),
            jax.ShapeDtypeStruct(moved, BF16),
        ),
        in_specs=[
            pl.BlockSpec((1, inner_size, width), by_outer),
            pl.BlockSpec((1, outer_size, width), by_inner),
            pl.BlockSpec((1, inner_size, inner_size), by_outer),
            pl.BlockSpec((1, outer_size, outer_size), by_inner),
            pl.BlockSpec(gate_weight.shape, whole),
        ],
        out_specs=(
            pl.BlockSpec((1, inner_size, width), by_back),
            pl.BlockSpec((1, inner_size, inner_size), by_back),
            pl.BlockSpec(gate_weight.shape, whole),
            pl.BlockSpec(memory_space=pl.ANY),
        ),
        scratch_shapes=[
            pltpu.VMEM(moved, BF16),
            pltpu.VMEM(moved, BF16),
            pltpu.VMEM((outer, inner_size, width), BF16),
            pltpu.VMEM((group, inner_size, width), BF16),
            pltpu.VMEM(moved, BF16),
        ] + [pltpu.SemaphoreType.DMA] * 6,
        compiler_params=pltpu.CompilerParams(
            collective_id=0, has_side_effects=True, vmem_limit_bytes=56 * 2**20
        ),
        name="exchange",
    )(tok3, back, first_factor, second_factor, gate_weight)
    gate_grad = lax.psum(gate_local, "seq")
    second_grad = pl.pallas_call(
        second_kernel,
        grid=(inner,),
        out_shape=jax.ShapeDtypeStruct(second_factor.shape, BF16),
        in_specs=[
            pl.BlockSpec((1, outer_size, width), lambda i: (i, 0, 0)),
            pl.BlockSpec((n, 1, outer, width), lambda i: (0, i, 0, 0)),
        ],
        out_specs=pl.BlockSpec((1, outer_size, outer_size), lambda i: (i, 0, 0)),
        compiler_params=pltpu.CompilerParams(vmem_limit_bytes=32 * 2**20),
        name="second",
    )(back, middle_here)
    return (
        token_grad.reshape(tokens.shape),
        first_grad,
        second_grad,
        gate_grad.astype(BF16),
    )


def solution(mesh):
    return jax.shard_map(
        functools.partial(on_device, mesh.shape["seq"]),
        mesh=mesh,
        in_specs=(
            P(("parts", "seq"), None),
            P(("parts", "seq"), None),
            P("seq", None, None),
            P("seq", None, None),
            P(),
        ),
        out_specs=(
            P(("parts", "seq"), None),
            P(("parts", "seq"), None, None),
            P(("parts", "seq"), None, None),
            P("parts", None),
        ),
        check_vma=False,
    )
```

time: 587 us -> 476 us (0.81)
  Pallas kernels: 0 us -> 384 us
  blocking collectives: 410 us -> 73.1 us
  matrix products: 105 us -> 0 us
  local copies, waits for them, and re-layouts: 62.8 us -> 16.3 us
    pallas_call x0 -> x2, Pallas kernels: none -> 384 us  [the longest x1 373 us: on_device(): pl.pallas_call(functools.partial(exchange_kernel, n, outer, inner, group)...]
    all_to_all x1 -> x0, blocking collectives: 190 us -> none  [on_device(): lax.all_to_all(middle_back, 'seq', split_axis=0, concat_axis=1, tiled=True)]
    psum x1, blocking collectives: 220 us -> 73.1 us  [on_device(): gate_grad = lax.psum(gate_local, 'seq')]
    dot_general x8 -> x0, matrix products: 105 us -> none  [the longest x1 22.4 us: on_device(): jnp.dot(tokens, gate_weight, preferred_element_type=jnp.float32)]
    convert_element_type x2 -> x0, local copies, waits for them, and re-layouts: 29.4 us -> none  [the longest x1 14.8 us: on_device(): middle_back = jnp.einsum('bak,bac->kbc', second_factor, back, preferred_e...]
    all_to_all x2 -> x0, local copies, waits for them, and re-layouts: 16.7 us -> none  [the longest x1 8.44 us: on_device(): lax.all_to_all(middle, 'seq', split_axis=0, concat_axis=1, tiled=True)]
    unnamed x6 -> x8, local copies, waits for them, and re-layouts: 16.7 us -> 16.3 us
  transfers between devices with their start and end apart: 1 -> 0, of which waited for: 0 -> 0; matrix products, arithmetic and copies ran while one was open for 7% -> 0% of each run, Pallas kernels for 0% -> 0%
where the time goes in v1:
time: 476 us; the launch traced here: 474 us
  Pallas kernels  384 us (81%)
  blocking collectives  73.1 us (15%)
  local copies, waits for them, and re-layouts  16.3 us (3%)
    pallas_call x1, Pallas kernels, on_device(): pl.pallas_call(functools.partial(exchange_kernel, n, outer, inner, group)...  373 us
    psum x1, blocking collectives, on_device(): gate_grad = lax.psum(gate_local, 'seq')  73.1 us
    unnamed x8, local copies, waits for them, and re-layouts  16.3 us
    pallas_call x1, Pallas kernels, on_device(): pl.pallas_call(second_kernel, grid=(inner,), out_shape=jax.ShapeDtypeStru...  10.9 us

profile of v1, /device:TPU:0, one launch (start us, length us, event | category | flops | bytes accessed | tf_op | source)
XLA Modules:
  0.0 473.7 jit_solution(2806099051781376574)
XLA Ops:
  0.6 372.8 %exchange.1 = (bf16[32,256,512]{2,1,0:T(8,128)(2,1)}, bf16[32,256,256]{2,1,0:T(8,128)(2,1)}, f32[512,512]{1,0:T(8,128)}, bf16[16,16,32,512]{3,2,1,0:T(8,128)(2,1)}) custom-call(bf16[32,256,512]{2,1,0:T(8,128)(2,1)} %bitcast.5, bf16[16,512,512]{2,1,0:T(8,128)(2,1)} %bitcast.3, bf16[32,256,256]{2,1,0:T(8,128)(2,1)} %ff_ref.1, bf16[16,512,512]{2,1,0:T(8,128)(2,1)} %sf_ref.1, ...), custom_call_target="tpu_custom_call" | custom-call | tf_op jit(solution)/shard_map/exchange/pallas_call | solution.py:194
  373.5 73.1 %all-reduce.1 = bf16[512,512]{1,0:T(8,128)(2,1)} all-reduce(f32[512,512]{1,0:T(8,128)} %get-tuple-element.11), channel_id=1, replica_groups=mesh['parts'=2,'seq'=16] {'seq'}, use_global_device_ids=true, to_apply=%region_0.0 | all-reduce | flops 262144 | bytes 1572864 | tf_op jit(solution)/shard_map/psum | solution.py:228
  446.5 0.0 copy-start
  446.5 3.4 copy-done
  449.9 0.0 copy-start.1
  449.9 3.4 copy-done.1
  453.3 10.9 %second.1 = bf16[16,512,512]{2,1,0:T(8,128)(2,1)} custom-call(bf16[16,512,512]{2,1,0:T(8,128)(2,1)S(1)} %bitcast.4, bf16[16,16,32,512]{3,2,1,0:T(8,128)(2,1)S(1)} %copy-done.1), custom_call_target="tpu_custom_call" | custom-call | tf_op jit(solution)/shard_map/second/pallas_call | solution.py:229
  464.2 0.0 copy-start.2
  464.2 7.5 %copy.13 = bf16[8192,512]{1,0:T(8,128)(2,1)} copy(bf16[8192,512]{1,0:T(8,128)(2,1)} %bitcast.6) | data formatting | bytes 16777216
  471.7 0.0 copy-done.2
  471.7 2.0 copy.14
Async XLA Ops:
  446.5 3.4 copy-start
  449.9 3.4 copy-start.1
  464.2 7.5 %copy-start.2 = (bf16[32,256,256]{2,1,0:T(8,128)(2,1)S(1)}, bf16[32,256,256]{2,1,0:T(8,128)(2,1)}, u32[]{:S(2)}) copy-start(bf16[32,256,256]{2,1,0:T(8,128)(2,1)} %get-tuple-element.17) | copy-start | bytes 12582916

commit v2 on v1

--- a/solution.py
+++ b/solution.py
@@ -28,28 +28,38 @@
 def exchange_kernel(
     n, outer, inner, group,
     tok_ref, cot_ref, ff_ref, sf_ref, w_ref,
-    tg_ref, fg_ref, gl_ref, mid_recv,
+    tg_ref, fg_ref, gg_ref, mid_recv,
     mb_send, mb_recv, mb_here, mid_group, mid_send,
+    gl_ref, slabs, own_slab, far_slab, gg_parts,
     mb_out, mb_in, mb_own, mid_out, mid_in, mid_own,
+    slab_out, slab_in, far_out, far_in, gg_out, gg_in,
 ):
     part, me = lax.axis_index("parts"), lax.axis_index("seq")
     step = pl.program_id(0)
     width = tok_ref.shape[2]
     inner_size = tok_ref.shape[1]
     batch = min(4, inner)
+    batches = inner // batch
     second, third = inner, inner + outer
     last = inner + 2 * outer - 1
     order = send_order(n)
 
-    def all_bytes(send, recv, out_sem, in_sem):
+    def remote(src, dst, out_sem, in_sem, to):
         return pltpu.make_async_remote_copy(
-            src_ref=send.at[pl.ds(0, n - 1)], dst_ref=recv.at[pl.ds(0, n - 1)],
-            send_sem=out_sem, recv_sem=in_sem,
-            device_id=(part, lax.rem(me + 1, n)), device_id_type=MESH,
+            src_ref=src, dst_ref=dst, send_sem=out_sem, recv_sem=in_sem,
+            device_id=(part, to), device_id_type=MESH,
         )
 
-    mb_all = all_bytes(mb_send, mb_recv, mb_out, mb_in)
-    mid_all = all_bytes(mid_send, mid_recv, mid_out, mid_in)
+    def mb_batch(k):
+        some = (pl.ds(0, n - 1), pl.ds(0, batch))
+        return remote(
+            mb_send.at[some], mb_recv.at[some], mb_out.at[k], mb_in.at[k], lax.rem(me + 1, n)
+        )
+
+    others = pl.ds(0, n - 1)
+    mid_all = remote(
+        mid_send.at[others], mid_recv.at[others], mid_out, mid_in, lax.rem(me + 1, n)
+    )
     mb_local = pltpu.make_async_copy(mb_send.at[me], mb_recv.at[me], mb_own)
     mid_local = pltpu.make_async_copy(mid_send.at[me], mid_recv.at[me], mid_own)
 
@@ -69,13 +79,12 @@
 
         @pl.when(lax.rem(step, batch) == batch - 1)
         def _():
+            k = step // batch
             rows = pl.ds(step - (batch - 1), batch)
             for s in order:
                 to = lax.rem(me + s, n)
-                pltpu.make_async_remote_copy(
-                    src_ref=mb_send.at[to, rows], dst_ref=mb_recv.at[me, rows],
-                    send_sem=mb_out, recv_sem=mb_in,
-                    device_id=(part, to), device_id_type=MESH,
+                remote(
+                    mb_send.at[to, rows], mb_recv.at[me, rows], mb_out.at[k], mb_in.at[k], to
                 ).start()
 
     @pl.when(step == second)
@@ -117,16 +126,15 @@
 
     @pl.when(step == third - 1)
     def _():
-        mb_all.wait_send()
+        for k in range(batches - 1):
+            mb_batch(k).wait_send()
         for s in order:
             to = lax.rem(me + s, n)
-            pltpu.make_async_remote_copy(
-                src_ref=mid_send.at[to], dst_ref=mid_recv.at[me],
-                send_sem=mid_out, recv_sem=mid_in,
-                device_id=(part, to), device_id_type=MESH,
-            ).start()
+            remote(mid_send.at[to], mid_recv.at[me], mid_out, mid_in, to).start()
         mid_local.start()
-        mb_all.wait_recv()
+        mb_batch(batches - 1).wait_send()
+        for k in range(batches):
+            mb_batch(k).wait_recv()
         mb_local.wait()
 
         def turn(j, carry):
@@ -154,12 +162,46 @@
 
     @pl.when(step == last)
     def _():
+        half = n // 2
+        mine, base = lax.rem(me, half), (me // half) * half
+        far = lax.rem(me + half, n)
+        tall_slab = width // half
+
+        def slab(i):
+            return gl_ref.at[pl.ds(pl.multiple_of(i * tall_slab, tall_slab), tall_slab)]
+
+        for s in range(1, half):
+            to = lax.rem(mine + s, half)
+            remote(slab(to), slabs.at[mine], slab_out, slab_in, base + to).start()
+        some = pl.ds(0, half - 1)
+        flat = pl.ds(0, (half - 1) * tall_slab)
+        sent = remote(gl_ref.at[flat], gl_ref.at[flat], slab_out, slab_in, far)
+        sent.wait_send()
+        remote(slabs.at[some], slabs.at[some], slab_out, slab_in, far).wait_recv()
+        total = slab(mine)[...]
+        for s in range(1, half):
+            total = total + slabs[lax.rem(mine + s, half)]
+        own_slab[...] = total
+        across = remote(own_slab, far_slab, far_out, far_in, far)
+        across.start()
+        across.wait()
+        gg_parts[mine] = (own_slab[...] + far_slab[...]).astype(BF16)
+        for s in range(1, half):
+            to = lax.rem(mine + s, half)
+            remote(gg_parts.at[mine], gg_parts.at[mine], gg_out, gg_in, base + to).start()
+        shared = remote(gg_parts.at[some], gg_parts.at[some], gg_out, gg_in, far)
+        shared.wait_send()
+        shared.wait_recv()
+        gg_ref[...] = gg_parts[...].reshape(width, width)
         mid_all.wait_send()
         mid_all.wait_recv()
         mid_local.wait()
 
 
-def second_kernel(cot_ref, mid_ref, sg_ref):
+def second_kernel(cot_ref, mid_ref, tg_ref, fg_ref, gg_ref, sg_ref, tg_out, fg_out, gg_out):
+    tg_out[...] = tg_ref[...]
+    fg_out[...] = fg_ref[...]
+    gg_out[...] = gg_ref[...]
     n, _, outer, width = mid_ref.shape
     middle = mid_ref[:, 0]
     if outer % 16:
@@ -176,6 +218,8 @@
     tok3 = tokens.reshape(outer, inner_size, width)
     back = cotangent.reshape(inner, outer_size, width)
     group = min(16, outer)
+    half = n // 2
+    batches = inner // min(4, inner)
     steps = inner + 2 * outer
 
     def by_inner(i):
@@ -191,13 +235,13 @@
         return (0, 0)
 
     moved = (n, inner, outer, width)
-    token_grad, first_grad, gate_local, middle_here = pl.pallas_call(
+    token_grad, first_grad, gate_grad, middle_here = pl.pallas_call(
         functools.partial(exchange_kernel, n, outer, inner, group),
         grid=(steps,),
         out_shape=(
             jax.ShapeDtypeStruct(tok3.shape, BF16),
             jax.ShapeDtypeStruct(first_factor.shape, BF16),
-            jax.ShapeDtypeStruct(gate_weight.shape, F32),
+            jax.ShapeDtypeStruct(gate_weight.shape, BF16),
             jax.ShapeDtypeStruct(moved, BF16),
         ),
         in_specs=[
@@ -219,31 +263,47 @@
             pltpu.VMEM((outer, inner_size, width), BF16),
             pltpu.VMEM((group, inner_size, width), BF16),
             pltpu.VMEM(moved, BF16),
-        ] + [pltpu.SemaphoreType.DMA] * 6,
+            pltpu.VMEM((width, width), F32),
+            pltpu.VMEM((half, width // half, width), F32),
+            pltpu.VMEM((width // half, width), F32),
+            pltpu.VMEM((width // half, width), F32),
+            pltpu.VMEM((half, width // half, width), BF16),
+        ] + [pltpu.SemaphoreType.DMA((batches,))] * 2 + [pltpu.SemaphoreType.DMA] * 10,
         compiler_params=pltpu.CompilerParams(
             collective_id=0, has_side_effects=True, vmem_limit_bytes=56 * 2**20
         ),
         name="exchange",
     )(tok3, back, first_factor, second_factor, gate_weight)
-    gate_grad = lax.psum(gate_local, "seq")
-    second_grad = pl.pallas_call(
+    per = outer // inner
+    tokens_spec = pl.BlockSpec((per, inner_size, width), lambda i: (i, 0, 0))
+    first_spec = pl.BlockSpec((per, inner_size, inner_size), lambda i: (i, 0, 0))
+    gate_spec = pl.BlockSpec(gate_weight.shape, whole)
+    second_grad, token_grad, first_grad, gate_grad = pl.pallas_call(
         second_kernel,
         grid=(inner,),
-        out_shape=jax.ShapeDtypeStruct(second_factor.shape, BF16),
+        out_shape=(
+            jax.ShapeDtypeStruct(second_factor.shape, BF16),
+            jax.ShapeDtypeStruct(tok3.shape, BF16),
+            jax.ShapeDtypeStruct(first_factor.shape, BF16),
+            jax.ShapeDtypeStruct(gate_weight.shape, BF16),
+        ),
         in_specs=[
             pl.BlockSpec((1, outer_size, width), lambda i: (i, 0, 0)),
             pl.BlockSpec((n, 1, outer, width), lambda i: (0, i, 0, 0)),
+            tokens_spec,
+            first_spec,
+            gate_spec,
         ],
-        out_specs=pl.BlockSpec((1, outer_size, outer_size), lambda i: (i, 0, 0)),
-        compiler_params=pltpu.CompilerParams(vmem_limit_bytes=32 * 2**20),
+        out_specs=(
+            pl.BlockSpec((1, outer_size, outer_size), lambda i: (i, 0, 0)),
+            tokens_spec,
+            first_spec,
+            gate_spec,
+        ),
+        compiler_params=pltpu.CompilerParams(vmem_limit_bytes=60 * 2**20),
         name="second",
-    )(back, middle_here)
-    return (
-        token_grad.reshape(tokens.shape),
-        first_grad,
-        second_grad,
-        gate_grad.astype(BF16),
-    )
+    )(back, middle_here, token_grad, first_grad, gate_grad)
+    return token_grad.reshape(tokens.shape), first_grad, second_grad, gate_grad
 
 
 def solution(mesh):

time: 476 us -> 411 us (0.86)
  blocking collectives: 73.1 us -> 0 us
  Pallas kernels: 384 us -> 409 us
  local copies, waits for them, and re-layouts: 16.3 us -> 0 us
    psum x1 -> x0, blocking collectives: 73.1 us -> none  [on_device(): gate_grad = lax.psum(gate_local, 'seq')]
    unnamed x8 -> x0, local copies, waits for them, and re-layouts: 16.3 us -> none
    pallas_call x1, Pallas kernels: 10.9 us -> 23.6 us  [on_device(): pl.pallas_call(second_kernel, grid=(inner,), out_shape=(jax.ShapeDtypeStr...]
    pallas_call x1, Pallas kernels: 373 us -> 385 us  [on_device(): pl.pallas_call(functools.partial(exchange_kernel, n, outer, inner, group)...]
where the time goes in v2:
time: 411 us; the launch traced here: 409 us
  Pallas kernels  409 us (100%)
    pallas_call x1, Pallas kernels, on_device(): pl.pallas_call(functools.partial(exchange_kernel, n, outer, inner, group)...  385 us
    pallas_call x1, Pallas kernels, on_device(): pl.pallas_call(second_kernel, grid=(inner,), out_shape=(jax.ShapeDtypeStr...  23.6 us

profile of v2, /device:TPU:0, one launch (start us, length us, event | category | flops | bytes accessed | tf_op | source)
XLA Modules:
  0.0 409.2 jit_solution(7844501510692628389)
XLA Ops:
  0.6 385.0 %exchange.1 = (bf16[32,256,512]{2,1,0:T(8,128)(2,1)}, bf16[32,256,256]{2,1,0:T(8,128)(2,1)}, bf16[512,512]{1,0:T(8,128)(2,1)}, bf16[16,16,32,512]{3,2,1,0:T(8,128)(2,1)}) custom-call(bf16[32,256,512]{2,1,0:T(8,128)(2,1)} %bitcast.5, bf16[16,512,512]{2,1,0:T(8,128)(2,1)} %bitcast.3, bf16[32,256,256]{2,1,0:T(8,128)(2,1)} %ff_ref.1, ...), custom_call_target="tpu_custom_call" | custom-call | tf_op jit(solution)/shard_map/exchange/pallas_call | solution.py:238
  385.6 23.6 %second.1 = (bf16[16,512,512]{2,1,0:T(8,128)(2,1)}, bf16[32,256,512]{2,1,0:T(8,128)(2,1)}, bf16[32,256,256]{2,1,0:T(8,128)(2,1)}, bf16[512,512]{1,0:T(8,128)(2,1)}) custom-call(bf16[16,512,512]{2,1,0:T(8,128)(2,1)} %bitcast.4, bf16[16,16,32,512]{3,2,1,0:T(8,128)(2,1)} %get-tuple-element.12.mid_ref, bf16[32,256,512]{2,1,0:T(8,128)(2,1)} %get-tuple-element.13.tg_ref, ...), custom_call_target="tpu_custom_call" | custom-call | tf_op jit(solution)/shard_map/second/pallas_call | solution.py:281

commit v3 on v2

--- a/solution.py
+++ b/solution.py
@@ -29,7 +29,7 @@
     n, outer, inner, group,
     tok_ref, cot_ref, ff_ref, sf_ref, w_ref,
     tg_ref, fg_ref, gg_ref, mid_recv,
-    mb_send, mb_recv, mb_here, mid_group, mid_send,
+    flat, spare, mb_recv, mid_group, mid_send,
     gl_ref, slabs, own_slab, far_slab, gg_parts,
     mb_out, mb_in, mb_own, mid_out, mid_in, mid_own,
     slab_out, slab_in, far_out, far_in, gg_out, gg_in,
@@ -51,17 +51,28 @@
         )
 
     def mb_batch(k):
-        some = (pl.ds(0, n - 1), pl.ds(0, batch))
-        return remote(
-            mb_send.at[some], mb_recv.at[some], mb_out.at[k], mb_in.at[k], lax.rem(me + 1, n)
-        )
+        some = mb_recv.at[pl.ds(0, n - 1), pl.ds(0, batch)]
+        return remote(some, some, mb_out.at[k], mb_in.at[k], lax.rem(me + 1, n))
 
     others = pl.ds(0, n - 1)
     mid_all = remote(
         mid_send.at[others], mid_recv.at[others], mid_out, mid_in, lax.rem(me + 1, n)
     )
+    mb_send = spare if outer % 16 else flat.reshape(n, inner, outer, width)
+    mb_here = flat.reshape(outer, inner_size, width)
     mb_local = pltpu.make_async_copy(mb_send.at[me], mb_recv.at[me], mb_own)
     mid_local = pltpu.make_async_copy(mid_send.at[me], mid_recv.at[me], mid_own)
+
+    def send_middle(start, stop, rows):
+        for s in order[start:stop]:
+            to = lax.rem(me + s, n)
+            remote(
+                mid_send.at[to, :, rows], mid_recv.at[me, :, rows], mid_out, mid_in, to
+            ).start()
+
+    first_rows = pl.ds(0, group)
+    other_rows = pl.ds(group, outer - group)
+    marks = [(n - 1) * k // 4 for k in (0, 2, 3, 4)]
 
     @pl.when(step == 0)
     def _():
@@ -128,9 +139,7 @@
     def _():
         for k in range(batches - 1):
             mb_batch(k).wait_send()
-        for s in order:
-            to = lax.rem(me + s, n)
-            remote(mid_send.at[to], mid_recv.at[me], mid_out, mid_in, to).start()
+        send_middle(0, n - 1, first_rows)
         mid_local.start()
         mb_batch(batches - 1).wait_send()
         for k in range(batches):
@@ -153,12 +162,18 @@
     @pl.when(step >= third)
     def _():
         tok, tok_f, gate, mixed = gated()
-        back = mb_here[step - third]
-        fg_ref[0] = dot(back, mixed, 1, 1).astype(BF16)
+        at = step - third
+        back = mb_here[at]
+        fg_ref[at] = dot(back, mixed, 1, 1).astype(BF16)
         mixed_back = dot(ff_ref[0], back, 0, 0)
         slope = (mixed_back * tok_f * gate * (1.0 - gate)).astype(BF16)
-        tg_ref[0] = (mixed_back * gate + dot(slope, w_ref[...], 1, 1)).astype(BF16)
+        tg_ref[at] = (mixed_back * gate + dot(slope, w_ref[...], 1, 1)).astype(BF16)
         gl_ref[...] += dot(tok, slope, 0, 0)
+
+    if outer > group:
+        @pl.when(step == third + outer // 2)
+        def _():
+            send_middle(marks[0], marks[1], other_rows)
 
     @pl.when(step == last)
     def _():
@@ -173,9 +188,11 @@
         for s in range(1, half):
             to = lax.rem(mine + s, half)
             remote(slab(to), slabs.at[mine], slab_out, slab_in, base + to).start()
+        if outer > group:
+            send_middle(marks[1], marks[2], other_rows)
         some = pl.ds(0, half - 1)
-        flat = pl.ds(0, (half - 1) * tall_slab)
-        sent = remote(gl_ref.at[flat], gl_ref.at[flat], slab_out, slab_in, far)
+        rows = pl.ds(0, (half - 1) * tall_slab)
+        sent = remote(gl_ref.at[rows], gl_ref.at[rows], slab_out, slab_in, far)
         sent.wait_send()
         remote(slabs.at[some], slabs.at[some], slab_out, slab_in, far).wait_recv()
         total = slab(mine)[...]
@@ -184,6 +201,8 @@
         own_slab[...] = total
         across = remote(own_slab, far_slab, far_out, far_in, far)
         across.start()
+        if outer > group:
+            send_middle(marks[2], marks[3], other_rows)
         across.wait()
         gg_parts[mine] = (own_slab[...] + far_slab[...]).astype(BF16)
         for s in range(1, half):
@@ -198,17 +217,42 @@
         mid_local.wait()
 
 
-def second_kernel(cot_ref, mid_ref, tg_ref, fg_ref, gg_ref, sg_ref, tg_out, fg_out, gg_out):
-    tg_out[...] = tg_ref[...]
-    fg_out[...] = fg_ref[...]
-    gg_out[...] = gg_ref[...]
+def second_kernel(
+    cot_ref, mid_ref, tg_ref, fg_ref, sg_ref, tg_out, fg_out, back, cot_sems, sems
+):
+    step, steps = pl.program_id(0), pl.num_programs(0)
     n, _, outer, width = mid_ref.shape
+    copies = [
+        pltpu.make_async_copy(tg_ref, tg_out, sems.at[0]),
+        pltpu.make_async_copy(fg_ref, fg_out, sems.at[1]),
+    ]
+    slot = lax.rem(step, 2)
+
+    def fetch(block, to):
+        return pltpu.make_async_copy(cot_ref.at[block], back.at[to], cot_sems.at[to])
+
+    @pl.when(step == 0)
+    def _():
+        fetch(0, 0).start()
+        for copy in copies:
+            copy.start()
+
+    @pl.when(step + 1 < steps)
+    def _():
+        fetch(step + 1, 1 - slot).start()
+
+    fetch(step, slot).wait()
     middle = mid_ref[:, 0]
     if outer % 16:
         middle = middle.astype(F32).reshape(n * outer, width).astype(BF16)
     else:
         middle = middle.reshape(n * outer, width)
-    sg_ref[0] = dot(cot_ref[0], middle, 1, 1).astype(BF16)
+    sg_ref[0] = dot(back[slot], middle, 1, 1).astype(BF16)
+
+    @pl.when(step == steps - 1)
+    def _():
+        for copy in copies:
+            copy.wait()
 
 
 def on_device(n, tokens, cotangent, first_factor, second_factor, gate_weight):
@@ -228,19 +272,17 @@
     def by_outer(i):
         return (lax.rem(jnp.maximum(i - inner, 0), outer), 0, 0)
 
-    def by_back(i):
-        return (jnp.maximum(i - inner - outer, 0), 0, 0)
-
     def whole(i):
         return (0, 0)
 
+    kept = pl.BlockSpec(memory_space=pltpu.VMEM)
     moved = (n, inner, outer, width)
     token_grad, first_grad, gate_grad, middle_here = pl.pallas_call(
         functools.partial(exchange_kernel, n, outer, inner, group),
         grid=(steps,),
         out_shape=(
-            jax.ShapeDtypeStruct(tok3.shape, BF16),
-            jax.ShapeDtypeStruct(first_factor.shape, BF16),
+            pltpu.VMEM(tok3.shape, BF16),
+            pltpu.VMEM(first_factor.shape, BF16),
             jax.ShapeDtypeStruct(gate_weight.shape, BF16),
             jax.ShapeDtypeStruct(moved, BF16),
         ),
@@ -252,15 +294,15 @@
             pl.BlockSpec(gate_weight.shape, whole),
         ],
         out_specs=(
-            pl.BlockSpec((1, inner_size, width), by_back),
-            pl.BlockSpec((1, inner_size, inner_size), by_back),
+            kept,
+            kept,
             pl.BlockSpec(gate_weight.shape, whole),
             pl.BlockSpec(memory_space=pl.ANY),
         ),
         scratch_shapes=[
+            pltpu.VMEM((outer * inner_size, width), BF16),
+            pltpu.VMEM(moved if outer % 16 else (16, LANES), BF16),
             pltpu.VMEM(moved, BF16),
-            pltpu.VMEM(moved, BF16),
-            pltpu.VMEM((outer, inner_size, width), BF16),
             pltpu.VMEM((group, inner_size, width), BF16),
             pltpu.VMEM(moved, BF16),
             pltpu.VMEM((width, width), F32),
@@ -270,39 +312,37 @@
             pltpu.VMEM((half, width // half, width), BF16),
         ] + [pltpu.SemaphoreType.DMA((batches,))] * 2 + [pltpu.SemaphoreType.DMA] * 10,
         compiler_params=pltpu.CompilerParams(
-            collective_id=0, has_side_effects=True, vmem_limit_bytes=56 * 2**20
+            collective_id=0, has_side_effects=True, vmem_limit_bytes=40 * 2**20
         ),
         name="exchange",
     )(tok3, back, first_factor, second_factor, gate_weight)
-    per = outer // inner
-    tokens_spec = pl.BlockSpec((per, inner_size, width), lambda i: (i, 0, 0))
-    first_spec = pl.BlockSpec((per, inner_size, inner_size), lambda i: (i, 0, 0))
-    gate_spec = pl.BlockSpec(gate_weight.shape, whole)
-    second_grad, token_grad, first_grad, gate_grad = pl.pallas_call(
+    second_grad, token_grad, first_grad = pl.pallas_call(
         second_kernel,
         grid=(inner,),
         out_shape=(
             jax.ShapeDtypeStruct(second_factor.shape, BF16),
             jax.ShapeDtypeStruct(tok3.shape, BF16),
             jax.ShapeDtypeStruct(first_factor.shape, BF16),
-            jax.ShapeDtypeStruct(gate_weight.shape, BF16),
         ),
         in_specs=[
-            pl.BlockSpec((1, outer_size, width), lambda i: (i, 0, 0)),
+            pl.BlockSpec(memory_space=pltpu.HBM),
             pl.BlockSpec((n, 1, outer, width), lambda i: (0, i, 0, 0)),
-            tokens_spec,
-            first_spec,
-            gate_spec,
+            kept,
+            kept,
         ],
         out_specs=(
             pl.BlockSpec((1, outer_size, outer_size), lambda i: (i, 0, 0)),
-            tokens_spec,
-            first_spec,
-            gate_spec,
-        ),
-        compiler_params=pltpu.CompilerParams(vmem_limit_bytes=60 * 2**20),
+            pl.BlockSpec(memory_space=pl.ANY),
+            pl.BlockSpec(memory_space=pl.ANY),
+        ),
+        scratch_shapes=[
+            pltpu.VMEM((2, outer_size, width), BF16),
+            pltpu.SemaphoreType.DMA((2,)),
+            pltpu.SemaphoreType.DMA((2,)),
+        ],
+        compiler_params=pltpu.CompilerParams(vmem_limit_bytes=8 * 2**20),
         name="second",
-    )(back, middle_here, token_grad, first_grad, gate_grad)
+    )(back, middle_here, token_grad, first_grad)
     return token_grad.reshape(tokens.shape), first_grad, second_grad, gate_grad
 
 

time: 411 us -> 401 us (0.976)
  Pallas kernels: 409 us -> 393 us
  local copies, waits for them, and re-layouts: 0 us -> 5.21 us
    pallas_call x1, Pallas kernels: 23.6 us -> 14.9 us  [on_device(): pl.pallas_call(second_kernel, grid=(inner,), out_shape=(jax.ShapeDtypeStr...]
    pallas_call x1, Pallas kernels: 385 us -> 378 us  [on_device(): pl.pallas_call(functools.partial(exchange_kernel, n, outer, inner, group)...]
    unnamed x0 -> x7, local copies, waits for them, and re-layouts: none -> 5.21 us
where the time goes in v3:
time: 401 us; the launch traced here: 399 us
  Pallas kernels  393 us (98%)
  local copies, waits for them, and re-layouts  5.21 us (1%)
    pallas_call x1, Pallas kernels, on_device(): pl.pallas_call(functools.partial(exchange_kernel, n, outer, inner, group)...  378 us
    pallas_call x1, Pallas kernels, on_device(): pl.pallas_call(second_kernel, grid=(inner,), out_shape=(jax.ShapeDtypeStr...  14.9 us

profile of v3, /device:TPU:0, one launch (start us, length us, event | category | flops | bytes accessed | tf_op | source)
XLA Modules:
  0.0 399.2 jit_solution(6683345571140480673)
XLA Ops:
  0.6 0.0 copy-start.2
  0.6 1.0 copy-done.2
  1.7 0.0 copy-start
  1.7 378.4 %exchange.1 = (bf16[32,256,512]{2,1,0:T(8,128)(2,1)S(1)}, bf16[32,256,256]{2,1,0:T(8,128)(2,1)S(1)}, bf16[512,512]{1,0:T(8,128)(2,1)S(1)}, bf16[16,16,32,512]{3,2,1,0:T(8,128)(2,1)}) custom-call(bf16[32,256,512]{2,1,0:T(8,128)(2,1)} %bitcast.5, bf16[16,512,512]{2,1,0:T(8,128)(2,1)} %bitcast.3, bf16[32,256,256]{2,1,0:T(8,128)(2,1)} %ff_ref.1, ...), custom_call_target="tpu_custom_call" | custom-call | tf_op jit(solution)/shard_map/exchange/pallas_call | solution.py:280
  380.1 0.0 copy-done
  380.1 0.0 copy-start.1
  380.1 3.4 copy-done.1
  383.5 14.9 %second.1 = (bf16[16,512,512]{2,1,0:T(8,128)(2,1)}, bf16[32,256,512]{2,1,0:T(8,128)(2,1)}, bf16[32,256,256]{2,1,0:T(8,128)(2,1)}) custom-call(bf16[16,512,512]{2,1,0:T(8,128)(2,1)S(1)} %bitcast.4, bf16[16,16,32,512]{3,2,1,0:T(8,128)(2,1)S(1)} %copy-done.1, bf16[32,256,512]{2,1,0:T(8,128)(2,1)S(1)} %get-tuple-element.12.tg_ref, ...), custom_call_target="tpu_custom_call" | custom-call | tf_op jit(solution)/shard_map/second/pallas_call | solution.py:319
  398.4 0.8 copy.10
Async XLA Ops:
  0.6 1.0 copy-start.2
  1.7 378.4 %copy-start = (bf16[8192,512]{1,0:T(8,128)(2,1)S(1)}, bf16[8192,512]{1,0:T(8,128)(2,1)}, u32[]{:S(2)}) copy-start(bf16[8192,512]{1,0:T(8,128)(2,1)} %param.6) | copy-start | bytes 25165828
  380.1 3.4 copy-start.1
